TPU v7x, 32 devices: a whole 2x2x4 slice. The times are simulated.
32 devices in a mesh: grp: 4 (over z), seq: 8 (over y, x, core).
Axes of the slice: x: 2, y: 2, z: 4, core: 2. Of those that a mesh axis runs over, the one named last changes fastest.
Arguments:
- queries: bfloat16 [4096, 6144], P(('grp', 'seq')), may hold values from -64 to 64
- keys_values: bfloat16 [4096, 768], P(('grp', 'seq')), may hold values from -6 to 6
- selection: int32 [64, 32], P(('grp', 'seq')), may hold values from -1 to 63, as said below
- gate_logits: bfloat16 [3, 4096, 32], P(None, ('grp', 'seq')), may hold values from -6 to 6
- pos_weight: bfloat16 [64, 384], replicated, may hold values from -0.75 to 0.75
- compress_weight: bfloat16 [384, 384], replicated, may hold values from -0.3125 to 0.3125
Outputs:
- attended: bfloat16 [4096, 6144], P(('grp', 'seq'))
Inputs may be any that keep to these rules, and one draw needn't show every extreme that they name: `selection`: A run is the 2 rows of one device; a segment is 16 consecutive rows. Row r lists, for each group, 16 distinct block numbers no greater than r, or -1 for unused entries. Within one group, the rows of a run list from each earlier segment exactly one block, and it lies in the run at the same place of that segment; from any other run of their own segment they list at most one block.
All inputs are finite; a program needn't handle non-finite values.
Results may differ from a plain program's by a relative error of at most 0.0055.
Values may be sent and summed in bfloat16 or wider, within the bound.
A program may use at most 128 MiB of HBM per device.

v0:
```python
import math
import jax
import jax.numpy as jnp
from jax import lax
from jax.sharding import PartitionSpec as P

HEAD_DIM = 192
GROUPS = 2
GROUP_HEADS = 16
HEADS = 32
BLOCK = 64
TOP = 16
CAP = 2
WINDOW = 128
NEG_FILL = -1e30


def from_behind(block, axis, distance):
    devices = range(lax.axis_size(axis))
    route = [(i - distance, i) for i in devices if i - distance in devices]
    return lax.ppermute(block, axis, route)


def attend(query_block, key_block, allowed, with_sink):
    head_dim = query_block.shape[-1]
    score_scale = head_dim ** (-0.5)
    scores = (
        jnp.einsum(
            "btghd,bgnd->bghtn",
            query_block,
            key_block[..., :head_dim],
            preferred_element_type=jnp.float32,
        )
        * score_scale
    )
    allowed_wide = allowed[:, :, None]
    scores = jnp.where(allowed_wide, scores, NEG_FILL)
    top_score = jnp.max(scores, axis=-1, keepdims=True)
    if with_sink:
        top_score = jnp.maximum(top_score, 0.0)
    weights = jnp.where(allowed_wide, jnp.exp(scores - top_score), 0.0)
    denominator = jnp.sum(weights, axis=-1, keepdims=True)
    if with_sink:
        denominator = denominator + jnp.exp(-top_score)
    rounded = weights.astype(jnp.bfloat16)
    blended = (
        jnp.einsum(
            "bghtn,bgnd->bghtd",
            rounded,
            key_block[..., head_dim:],
            preferred_element_type=jnp.float32,
        )
        / denominator
    )
    return jnp.transpose(blended, (0, 3, 1, 2, 4))


def by_heads(query_block, key_block, allowed, with_sink):
    head_count = query_block.shape[3]
    slab_width = math.gcd(4, head_count)

    def head_slab(slab_index):
        query_slab = lax.dynamic_slice_in_dim(query_block, slab_index * slab_width, slab_width, 3)
        return attend(query_slab, key_block, allowed, with_sink)

    stacked = lax.map(head_slab, jnp.arange(head_count // slab_width, dtype=jnp.int32))
    stacked = jnp.moveaxis(stacked, 0, 3)
    return stacked.reshape(stacked.shape[:3] + (head_count, stacked.shape[-1]))


def compress_blocks(keys_values, pos_weight, compress_weight):
    block_count = keys_values.shape[0] // BLOCK
    grouped = keys_values.reshape(block_count, BLOCK, GROUPS, 2 * HEAD_DIM).astype(jnp.float32)
    pooled = jnp.sum(grouped * pos_weight.astype(jnp.float32)[None, :, None, :], axis=1).astype(
        jnp.bfloat16
    )
    mapped = jnp.dot(
        pooled.reshape(block_count * GROUPS, 2 * HEAD_DIM),
        compress_weight,
        preferred_element_type=jnp.float32,
    )
    return mapped.astype(jnp.bfloat16).reshape(block_count, GROUPS, 2 * HEAD_DIM)


def plan_requests(unit_of, key_of, wanted, unit_count, key_count):
    hits = (
        wanted[:, None, None]
        & (unit_of[:, None, None] == jnp.arange(unit_count, dtype=jnp.int32)[None, :, None])
        & (key_of[:, None, None] == jnp.arange(key_count, dtype=jnp.int32)[None, None, :])
    )
    present = jnp.any(hits, axis=0)
    ordinal = jnp.cumsum(present.astype(jnp.int32), axis=1) - 1
    slot_of = jnp.sum(jnp.where(hits, ordinal[None], 0), axis=(1, 2))
    matches = present[:, :, None] & (
        ordinal[:, :, None] == jnp.arange(CAP, dtype=jnp.int32)[None, None, :]
    )
    requests = (
        jnp.sum(
            jnp.where(matches, jnp.arange(key_count, dtype=jnp.int32)[None, :, None] + 1, 0), axis=1
        )
        - 1
    )
    return (slot_of, requests)


def shards(queries, keys_values, selection, gate_logits, pos_weight, compress_weight):
    grp_index = lax.axis_index("grp")
    seq_index = lax.axis_index("seq")
    grp_count = lax.axis_size("grp")
    seq_count = lax.axis_size("seq")
    tok_count = queries.shape[0]
    dev_blocks = tok_count // BLOCK
    seg_tokens = tok_count * seq_count
    seg_blocks = seg_tokens // BLOCK
    all_blocks = seg_blocks * grp_count
    key_count = GROUPS * dev_blocks
    first_pos = (grp_index * seq_count + seq_index) * tok_count
    positions = first_pos + jnp.arange(tok_count, dtype=jnp.int32)
    local_view = keys_values.reshape(dev_blocks, BLOCK, GROUPS, 2 * HEAD_DIM)
    local_summary = jnp.transpose(
        compress_blocks(keys_values, pos_weight, compress_weight), (1, 0, 2)
    )
    summaries = lax.all_gather(local_summary, ("grp", "seq"), axis=1, tiled=True)
    picked = selection.reshape(dev_blocks, GROUPS, TOP)
    group_ids = jnp.broadcast_to(jnp.arange(GROUPS, dtype=jnp.int32)[None, :, None], picked.shape)
    flat_groups = group_ids.reshape(-1)
    flat_picks = picked.reshape(-1)
    clipped_flat = jnp.maximum(flat_picks, 0)
    segment_of = clipped_flat // seg_blocks
    key_of = flat_groups * dev_blocks + clipped_flat % dev_blocks
    wanted = (flat_picks >= 0) & (segment_of != grp_index)
    slot_of, requests = plan_requests(segment_of, key_of, wanted, grp_count, key_count)
    asked_clipped = jnp.maximum(
        lax.all_to_all(requests, "grp", split_axis=0, concat_axis=0, tiled=True), 0
    )
    received = lax.all_to_all(
        local_view[asked_clipped % dev_blocks, :, asked_clipped // dev_blocks, :],
        "grp",
        split_axis=0,
        concat_axis=0,
        tiled=True,
    )
    picks_clipped = jnp.maximum(picked, 0)
    pick_segment = picks_clipped // seg_blocks
    from_remote = received[pick_segment, slot_of.reshape(picked.shape)]
    segment = lax.all_gather(keys_values, "seq", axis=0, tiled=True)
    earlier_tail = from_behind(segment[seg_tokens - WINDOW :], "grp", 1)
    segment_view = segment.reshape(seg_blocks, BLOCK, GROUPS, 2 * HEAD_DIM)
    from_segment = segment_view[picks_clipped % seg_blocks, :, group_ids, :]
    start_row = jnp.maximum(seq_index * tok_count - WINDOW, 0)
    inside = lax.dynamic_slice_in_dim(segment, start_row, WINDOW, 0)
    before = jnp.where(seq_index == 0, earlier_tail, inside)
    own_rows = (pick_segment == grp_index)[..., None, None]
    chosen = jnp.where(own_rows, from_segment, from_remote).reshape(
        dev_blocks, GROUPS, TOP * BLOCK, 2 * HEAD_DIM
    )
    key_positions = (picks_clipped[..., None] * BLOCK + jnp.arange(BLOCK, dtype=jnp.int32)).reshape(
        dev_blocks, GROUPS, TOP * BLOCK
    )
    live_keys = jnp.repeat(picked >= 0, BLOCK, axis=2)
    block_positions = positions.reshape(dev_blocks, BLOCK)
    allowed_sel = live_keys[:, :, None, :] & (
        key_positions[:, :, None, :] <= block_positions[:, None, :, None]
    )
    query_blocks = queries.reshape(dev_blocks, BLOCK, GROUPS, GROUP_HEADS, HEAD_DIM)
    selected_branch = by_heads(query_blocks, chosen, allowed_sel, False).reshape(
        tok_count, GROUPS, GROUP_HEADS, HEAD_DIM
    )
    query_whole = queries.reshape(1, tok_count, GROUPS, GROUP_HEADS, HEAD_DIM)
    block_ends = jnp.arange(all_blocks, dtype=jnp.int32) * BLOCK + BLOCK - 1
    allowed_comp = (block_ends[None, :] <= positions[:, None])[None, None]
    compressed_branch = by_heads(query_whole, summaries[None], allowed_comp, True)[0]
    nearby = jnp.concatenate([before, keys_values], axis=0).reshape(
        WINDOW + tok_count, GROUPS, 2 * HEAD_DIM
    )
    nearby = jnp.transpose(nearby, (1, 0, 2))[None]
    near_positions = first_pos - WINDOW + jnp.arange(WINDOW + tok_count, dtype=jnp.int32)
    allowed_win = (
        (near_positions[None, :] <= positions[:, None])
        & (near_positions[None, :] > positions[:, None] - WINDOW)
        & (near_positions[None, :] >= 0)
    )[None, None]
    window_branch = by_heads(query_whole, nearby, allowed_win, False)[0]
    gate_values = jax.nn.sigmoid(gate_logits.astype(jnp.float32)).reshape(
        3, tok_count, GROUPS, GROUP_HEADS, 1
    )
    attended = (
        gate_values[0] * compressed_branch
        + gate_values[1] * selected_branch
        + gate_values[2] * window_branch
    )
    return attended.reshape(tok_count, HEADS * HEAD_DIM).astype(jnp.bfloat16)


def solution(mesh):
    in_specs = (
        P(("grp", "seq"), None),
        P(("grp", "seq"), None),
        P(("grp", "seq"), None),
        P(None, ("grp", "seq"), None),
        P(),
        P(),
    )
    out_specs = P(("grp", "seq"), None)
    return jax.shard_map(shards, mesh=mesh, in_specs=in_specs, out_specs=out_specs, check_vma=False)
```

profile of v0, /device:TPU:0, one launch (start us, length us, event | category | flops | bytes accessed | tf_op | source)
XLA Modules:
  0.0 216.7 jit_solution(13625318544058351301)
XLA Ops:
  10.9 6.3 %all-to-all-start = ((s32[4,1,2]{2,1,0:T(1,128)}), s32[4,1,2]{2,1,0:T(1,128)}, u32[]{:S(2)}, u32[]{:S(2)}) async-start(s32[4,1,2]{2,1,0:T(1,128)} %copy.101), calls=%async_computation | async-start | bytes 4096 | tf_op jit(solution)/shard_map/all_to_all | solution.py:134
  18.9 2.6 %copy.97 = bf16[128,6144]{0,1:T(8,128)(2,1)} copy(bf16[128,6144]{1,0:T(8,128)(2,1)} %param.12) | data formatting | bytes 3145728 | tf_op args[0]
  22.0 42.4 %all_gather.6 = bf16[2,64,384]{2,0,1:T(2,128)(2,1)S(1)} all-gather(bf16[2,2,384]{2,0,1:T(2,128)(2,1)S(1)} %bitcast.261), channel_id=1, replica_groups=mesh['grp'=4,'seq'=8] {'grp','seq'}, dimensions={1}, use_global_device_ids=true | all-gather | bytes 101376 | tf_op jit(solution)/shard_map/all_gather | solution.py:123
  65.3 14.9 %while.33 = (s32[]{:T(128)}, f32[4,1,128,2,4,192]{2,5,4,0,3,1:T(8,128)S(1)}, s32[4]{0:T(128)}, bf16[1,128,2,16,192]{1,4,3,2,0:T(8,128)(2,1)}, bf16[1,2,64,384]{3...) while((s32[]{:T(128)}, ...), condition=%wide.region_4.5_spmd.clone, body=%wide.region_1.4_spmd.clone.sunk | while | flops 51128324 | bytes 2171823 | solution.py:66
  80.3 1.8 copy.106
  87.3 2.3 %gather_fusion.1 = bf16[8,64,384]{2,1,0:T(8,128)(2,1)} fusion(bf16[2,64,2,384]{3,1,2,0:T(8,128)(2,1)} %copy.106, s32[8]{0:T(128)S(1)} %reshape.547), kind=kCustom, calls=%fused_computation.1 | custom fusion | bytes 786496 | tf_op jit(solution)/shard_map/gather | solution.py:137
  89.6 3.5 %all-to-all-start.1 = ((bf16[4,2,64,384]{3,2,1,0:T(8,128)(2,1)}), bf16[4,2,64,384]{3,2,1,0:T(8,128)(2,1)S(1)}, u32[]{:S(2)}, u32[]{:S(2)}) async-start(bf16[4,2,64,384]{3,2,1,0:T(8,128)(2,1)} %bitcast.255), calls=%async_computation.1 | async-start | bytes 786432 | tf_op jit(solution)/shard_map/all_to_all | solution.py:136
  93.8 4.7 %reshape.537 = bf16[2,64,2,16,192]{4,3,2,1,0:T(8,128)(2,1)} reshape(bf16[128,6144]{1,0:T(8,128)(2,1)} %param.12) | data formatting | bytes 3145728 | tf_op jit(solution)/shard_map/reshape | solution.py:165
  99.1 6.4 %all-to-all-done.1 = bf16[4,2,64,384]{3,2,1,0:T(8,128)(2,1)S(1)} async-done(((bf16[4,2,64,384]{3,2,1,0:T(8,128)(2,1)}), bf16[4,2,64,384]{3,2,1,0:T(8,128)(2,1)S(1)}, u32[]{:S(2)}, u32[]{:S(2)}) %all-to-all-start.1) | async-done | bytes 393248 | tf_op jit(solution)/shard_map/all_to_all | solution.py:136
  105.5 2.7 %gather_fusion.2 = bf16[64,64,384]{2,1,0:T(8,128)(2,1)} fusion(bf16[4,2,64,384]{3,2,1,0:T(8,128)(2,1)S(1)} %all-to-all-done.1, s32[64]{0:T(128)S(1)} %reshape.553), kind=kCustom, calls=%fused_computation.2 | custom fusion | bytes 6291968 | tf_op jit(solution)/shard_map/gather | solution.py:145
  108.2 3.4 %reshape.538 = bf16[16,64,2,384]{3,2,1,0:T(2,128)(2,1)S(1)} reshape(bf16[1024,768]{1,0:T(8,128)(2,1)} %all-gather.2.cloned.1.call-done) | data formatting | bytes 3145728 | tf_op jit(solution)/shard_map/reshape | solution.py:148
  111.9 2.7 %gather_fusion = bf16[64,64,384]{2,1,0:T(8,128)(2,1)} fusion(bf16[16,64,2,384]{3,1,2,0:T(8,128)(2,1)S(1)} %copy.100, s32[64]{0:T(128)S(1)} %reshape.541), kind=kCustom, calls=%fused_computation | custom fusion | bytes 6291968 | tf_op jit(solution)/shard_map/gather | solution.py:149
  114.6 4.4 %broadcast_select_fusion = bf16[2,2,1024,384]{3,2,1,0:T(8,128)(2,1)} fusion(bf16[2,2,1024,384]{3,2,1,0:T(8,128)(2,1)} %bitcast.253, bf16[2,2,1024,384]{3,2,1,0:T(8,128)(2,1)} %bitcast.252, pred[2,2,1024]{2,1,0:T(4,128)(4,1)S(1)} %broadcast_in_dim.161), kind=kLoop, calls=%fused_computation.84 | loop fusion | flops 1572864 | bytes 9441280 | tf_op jit(solution)/shard_map/jit(_where)/select_n | solution.py:154
  119.0 3.2 %copy.108 = bf16[2,2,1024,384]{2,3,1,0:T(8,128)(2,1)S(1)} copy(bf16[2,2,1024,384]{3,2,1,0:T(8,128)(2,1)} %broadcast_select_fusion) | data formatting | bytes 6291456
  123.8 2.1 collective-permute-start
  125.9 30.6 %while.34 = (s32[]{:T(128)}, f32[4,2,64,2,4,192]{5,2,4,3,1,0:T(8,128)}, s32[4]{0:T(128)S(1)}, bf16[2,64,2,16,192]{4,3,2,1,0:T(8,128)(2,1)}, bf16[2,2,1024,384]{2...) while((s32[]{:T(128)}, ...), condition=%wide.region_12.13_spmd.clone, body=%wide.region_9.12_spmd.clone.sunk | while | flops 814416896 | bytes 18646196 | solution.py:66
  129.6 2.1 fusion.132
  137.3 2.1 fusion.132
  144.9 2.1 fusion.132
  147.0 1.8 fusion.133
  152.6 2.1 fusion.132
  156.4 11.7 %copy.121 = f32[2,64,2,4,4,192]{1,0,5,4,3,2:T(2,128)} copy(f32[2,64,2,4,4,192]{5,1,4,2,0,3:T(8,128)} %bitcast.16) | data formatting | bytes 6291456 | tf_op jit(solution)/shard_map/reshape;reshape | solution.py:166
  168.1 5.8 %reshape.575 = f32[128,6144]{0,1:T(8,128)S(1)} reshape(f32[2,64,2,4,4,192]{1,0,5,4,3,2:T(2,128)} %copy.121) | data formatting | bytes 6291456 | tf_op jit(solution)/shard_map/reshape;reshape | solution.py:166
  176.8 1.9 copy.111
  178.7 2.0 broadcast.656.clone2
  180.7 21.9 %while.35 = (s32[]{:T(128)}, f32[4,1,128,2,4,192]{2,5,4,0,3,1:T(8,128)}, s32[4]{0:T(128)S(1)}, bf16[1,128,2,16,192]{1,4,3,2,0:T(8,128)(2,1)}, bf16[1,2,256,384]{...) while((s32[]{:T(128)}, ...), condition=%wide.region_16.17_spmd.clone, body=%wide.region_13.16_spmd.clone.sunk | while | flops 204011520 | bytes 4873147 | solution.py:66
  184.0 2.2 %fusion.138 = f32[4,1,128,2,4,192]{2,5,4,0,3,1:T(8,128)} fusion(f32[4,1,128,2,4,192]{2,5,4,0,3,1:T(8,128)} %get-tuple-element.488, s32[]{:T(128)} %get-tuple-element.487, f32[1,2,4,128,256]{4,3,2,1,0:T(8,128)S(1)} %get-tuple-element.472, f32[2,4,128]{2,1,0:T(4,128)S(1)} %get-tuple-element.473, pred[128,256]{1,0:T(8,128)(4,1)S(1)} %and_and_fusion.2, ...), kind=kOutput, calls=%fused_computation.60.clone.1 | convolution fusion | flops 101646336 | bytes 2073088 | tf_op jit(solution)/shard_map/while/body/eval_jaxpr/bghtn,bgnd->bghtd/dot_general | solution.py:47
  189.4 2.2 %fusion.138 = f32[4,1,128,2,4,192]{2,5,4,0,3,1:T(8,128)} fusion(f32[4,1,128,2,4,192]{2,5,4,0,3,1:T(8,128)} %get-tuple-element.488, s32[]{:T(128)} %get-tuple-element.487, f32[1,2,4,128,256]{4,3,2,1,0:T(8,128)S(1)} %get-tuple-element.472, f32[2,4,128]{2,1,0:T(4,128)S(1)} %get-tuple-element.473, pred[128,256]{1,0:T(8,128)(4,1)S(1)} %and_and_fusion.2, ...), kind=kOutput, calls=%fused_computation.60.clone.1 | convolution fusion | flops 101646336 | bytes 2073088 | tf_op jit(solution)/shard_map/while/body/eval_jaxpr/bghtn,bgnd->bghtd/dot_general | solution.py:47
  194.9 2.2 %fusion.138 = f32[4,1,128,2,4,192]{2,5,4,0,3,1:T(8,128)} fusion(f32[4,1,128,2,4,192]{2,5,4,0,3,1:T(8,128)} %get-tuple-element.488, s32[]{:T(128)} %get-tuple-element.487, f32[1,2,4,128,256]{4,3,2,1,0:T(8,128)S(1)} %get-tuple-element.472, f32[2,4,128]{2,1,0:T(4,128)S(1)} %get-tuple-element.473, pred[128,256]{1,0:T(8,128)(4,1)S(1)} %and_and_fusion.2, ...), kind=kOutput, calls=%fused_computation.60.clone.1 | convolution fusion | flops 101646336 | bytes 2073088 | tf_op jit(solution)/shard_map/while/body/eval_jaxpr/bghtn,bgnd->bghtd/dot_general | solution.py:47
  200.4 2.3 %fusion.138 = f32[4,1,128,2,4,192]{2,5,4,0,3,1:T(8,128)} fusion(f32[4,1,128,2,4,192]{2,5,4,0,3,1:T(8,128)} %get-tuple-element.488, s32[]{:T(128)} %get-tuple-element.487, f32[1,2,4,128,256]{4,3,2,1,0:T(8,128)S(1)} %get-tuple-element.472, f32[2,4,128]{2,1,0:T(4,128)S(1)} %get-tuple-element.473, pred[128,256]{1,0:T(8,128)(4,1)S(1)} %and_and_fusion.2, ...), kind=kOutput, calls=%fused_computation.60.clone.1 | convolution fusion | flops 101646336 | bytes 2073088 | tf_op jit(solution)/shard_map/while/body/eval_jaxpr/bghtn,bgnd->bghtd/dot_general | solution.py:47
  202.6 4.6 %fusion.84 = bf16[128,6144]{0,1:T(8,128)(2,1)} fusion(f32[4,1,128,2,4,192]{2,5,4,0,3,1:T(8,128)} %get-tuple-element.103, f32[4,1,128,2,4,192]{2,5,4,0,3,1:T(8,128)} %copy-done.1, f32[128,6144]{0,1:T(8,128)S(1)} %reshape.575, f32[128,2,16]{0,2,1:T(8,128)S(1)} %bitcast.259, f32[128,2,16]{0,2,1:T(8,128)S(1)} %bitcast.260, f32[128,2,16]{0,2,1:T(8,128)S(1)} %bitcast.258), kind=kLoop, calls=%fused_computation.80 | loop fusion | flops 4718592 | bytes 11059200 | tf_op jit(solution)/shard_map/convert_element_type | solution.py:192
  207.3 2.6 %copy.113 = bf16[128,6144]{1,0:T(8,128)(2,1)} copy(bf16[128,6144]{0,1:T(8,128)(2,1)} %fusion.84) | data formatting | bytes 3145728 | tf_op jit(solution)/shard_map/convert_element_type | solution.py:192
  (155 shorter events, 58.9 us)
Async XLA Ops:
  6.5 15.3 %copy-start = (bf16[384,384]{1,0:T(8,128)(2,1)S(1)}, bf16[384,384]{1,0:T(8,128)(2,1)}, u32[]{:S(2)}) copy-start(bf16[384,384]{1,0:T(8,128)(2,1)} %param.17) | copy-start | bytes 884740
  6.5 15.0 %copy-start.3 = (bf16[64,384]{1,0:T(8,128)(2,1)S(1)}, bf16[64,384]{1,0:T(8,128)(2,1)}, u32[]{:S(2)}) copy-start(bf16[64,384]{1,0:T(8,128)(2,1)} %param.16) | copy-start | bytes 147460
  9.1 8.1 %copy-start.7 = (pred[2,32]{1,0:T(4,128)(4,1)}, pred[2,32]{1,0:T(4,128)(4,1)S(1)}, u32[]{:S(2)}) copy-start(pred[2,32]{1,0:T(4,128)(4,1)S(1)} %get-tuple-element.310) | copy-start | bytes 196
  9.1 8.1 %copy-start.8 = (pred[2,32]{1,0:T(4,128)(4,1)}, pred[2,32]{1,0:T(4,128)(4,1)S(1)}, u32[]{:S(2)}) copy-start(pred[2,32]{1,0:T(4,128)(4,1)S(1)} %get-tuple-element.293) | copy-start | bytes 196
  9.5 0.5 copy-start.5
  9.5 12.5 %copy-start.6 = (pred[64,4]{0,1:T(4,128)(4,1)}, pred[64,4]{0,1:T(4,128)(4,1)S(1)}, u32[]{:S(2)}) copy-start(pred[64,4]{0,1:T(4,128)(4,1)S(1)} %get-tuple-element.312) | copy-start | bytes 772
  10.9 75.5 %all-to-all-start = ((s32[4,1,2]{2,1,0:T(1,128)}), s32[4,1,2]{2,1,0:T(1,128)}, u32[]{:S(2)}, u32[]{:S(2)}) async-start(s32[4,1,2]{2,1,0:T(1,128)} %copy.101), calls=%async_computation | async-start | bytes 4096 | tf_op jit(solution)/shard_map/all_to_all | solution.py:134
  17.2 91.0 %all-gather.2.cloned.1.call-start = ((), (), s32[]{:S(2)}) async-start(), calls=%async_computation.2 | async-start | bytes 1769472 | tf_op jit(solution)/shard_map/all_gather | solution.py:146
  18.9 45.5 %copy-start.2 = (bf16[2,64,2,384]{3,2,1,0:T(2,128)(2,1)}, bf16[2,64,2,384]{3,2,1,0:T(2,128)(2,1)S(1)}, u32[]{:S(2)}) copy-start(bf16[2,64,2,384]{3,2,1,0:T(2,128)(2,1)S(1)} %reshape.535) | copy-start | bytes 589828
  80.2 9.4 %copy-start.1 = (f32[4,1,128,2,4,192]{2,5,4,0,3,1:T(8,128)}, f32[4,1,128,2,4,192]{2,5,4,0,3,1:T(8,128)S(1)}, u32[]{:S(2)}) copy-start(f32[4,1,128,2,4,192]{2,5,4,0,3,1:T(8,128)S(1)} %get-tuple-element.101) | copy-start | bytes 9437188
  80.2 18.9 %copy-start.4 = (bf16[3,128,32]{1,2,0:T(8,128)(2,1)S(1)}, bf16[3,128,32]{1,2,0:T(8,128)(2,1)}, u32[]{:S(2)}) copy-start(bf16[3,128,32]{1,2,0:T(8,128)(2,1)} %param.15) | copy-start | bytes 73732
  89.6 15.9 %all-to-all-start.1 = ((bf16[4,2,64,384]{3,2,1,0:T(8,128)(2,1)}), bf16[4,2,64,384]{3,2,1,0:T(8,128)(2,1)S(1)}, u32[]{:S(2)}, u32[]{:S(2)}) async-start(bf16[4,2,64,384]{3,2,1,0:T(8,128)(2,1)} %bitcast.255), calls=%async_computation.1 | async-start | bytes 786432 | tf_op jit(solution)/shard_map/all_to_all | solution.py:136
  123.8 50.2 %collective-permute-start = (bf16[128,768]{1,0:T(8,128)(2,1)}, bf16[128,768]{1,0:T(8,128)(2,1)}, u32[]{:S(2)}, u32[]{:S(2)}) collective-permute-start(bf16[128,768]{1,0:T(8,128)(2,1)} %slice.52), channel_id=1, source_target_pairs={{0,8},{8,16},{16,24},{1,9},{9,17},{17,25},{2,10},{10,18},{18,26},{... | collective-permute-start | bytes 589832 | tf_op jit(solution)/shard_map/ppermute | solution.py:21
Sparse Core Ops, SparseCore 0:
  19.9 27.4 all-gather.1
where the time goes:
time: 218 us; the launch traced here: 217 us
  local copies, waits for them, and re-layouts  74.2 us (34%)
  blocking collectives  42.4 us (19%)
  matrix products  31.7 us (15%)
  other arithmetic  28.2 us (13%)
  between operations  13.7 us (6%)
  starting transfers between devices  11.9 us (5%)
  loops' own time  7.63 us (4%)
  waiting for transfers between devices  7.09 us (3%)
    all_gather x1, blocking collectives, shards(): lax.all_gather(local_summary, ('grp', 'seq'), axis=1, tiled=True)  42.4 us
    dot_general x12, matrix products, attend(): jnp.einsum('bghtn,bgnd->bghtd', rounded, key_block[..., head_dim:], prefe...  17.7 us
    another operation x2, local copies, waits for them, and re-layouts, shards(): by_heads(query_blocks, chosen, allowed_sel, False)  17.5 us
    dot_general x12, matrix products, attend(): jnp.einsum('btghd,bgnd->bghtn', query_block, key_block[..., :head_dim], p...  13.8 us
    dynamic_slice x12, local copies, waits for them, and re-layouts, by_heads(): lax.map(head_slab, jnp.arange(head_count // slab_width, dtype=jnp.int32))  9.99 us
    sub x4, other arithmetic, attend(): weights = jnp.where(allowed_wide, jnp.exp(scores - top_score), 0.0)  8.59 us
    another operation x3, loops' own time, by_heads(): lax.map(head_slab, jnp.arange(head_count // slab_width, dtype=jnp.int32))  7.63 us
    all_to_all x1, waiting for transfers between devices, shards(): lax.all_to_all(local_view[asked_clipped % dev_blocks, :, asked_clipped //...  6.38 us
  transfers between devices with their start and end apart: 4, of which 1 were waited for; matrix products, arithmetic and copies ran while one was open for 37% of the time, Pallas kernels for 0%

commit v1 on v0

--- a/solution.py
+++ b/solution.py
@@ -13,6 +13,29 @@
 CAP = 2
 WINDOW = 128
 NEG_FILL = -1e30
+
+
+def cut_along(x, dim, devices):
+    shape = x.shape
+    pieces = x.reshape(*shape[:dim], devices, shape[dim] // devices, *shape[dim + 1 :])
+    return jnp.moveaxis(pieces, dim, 0)
+
+
+def joined_along(blocks, dim):
+    lengths = list(blocks.shape[1:])
+    lengths[dim] *= blocks.shape[0]
+    return jnp.moveaxis(blocks, 0, dim).reshape(lengths)
+
+
+def swapped_with_each(shard, axis, split_dim, concat_dim):
+    size, index = (lax.axis_size(axis), lax.axis_index(axis))
+    tiles = cut_along(shard, split_dim, size)
+    outs = [tiles[index]]
+    for turn in range(1, size):
+        sent = tiles[index ^ turn]
+        outs.append(lax.ppermute(sent, axis, [(i, i ^ turn) for i in range(size)]))
+    tiles = jnp.stack(outs)[index ^ jnp.arange(size)]
+    return joined_along(tiles, concat_dim)
 
 
 def from_behind(block, axis, distance):
@@ -130,9 +153,7 @@
     key_of = flat_groups * dev_blocks + clipped_flat % dev_blocks
     wanted = (flat_picks >= 0) & (segment_of != grp_index)
     slot_of, requests = plan_requests(segment_of, key_of, wanted, grp_count, key_count)
-    asked_clipped = jnp.maximum(
-        lax.all_to_all(requests, "grp", split_axis=0, concat_axis=0, tiled=True), 0
-    )
+    asked_clipped = jnp.maximum(swapped_with_each(requests, "grp", 0, 0), 0)
     received = lax.all_to_all(
         local_view[asked_clipped % dev_blocks, :, asked_clipped // dev_blocks, :],
         "grp",

time: 218 us -> 223 us (1.023)
  other arithmetic: 28.2 us -> 31.9 us
    all_to_all x1 -> x0, starting transfers between devices: 6.32 us -> none  [shards(): lax.all_to_all(requests, 'grp', split_axis=0, concat_axis=0, tiled=True)]
    ppermute x0 -> x3, starting transfers between devices: none -> 5.62 us  [swapped_with_each(): outs.append(lax.ppermute(sent, axis, [(i, i ^ turn) for i in range(size)]))]
    ppermute x0 -> x3, other arithmetic: none -> 2.38 us  [swapped_with_each(): outs.append(lax.ppermute(sent, axis, [(i, i ^ turn) for i in range(size)]))]
  transfers between devices with their start and end apart: 4 -> 6, of which waited for: 1 -> 1; matrix products, arithmetic and copies ran while one was open for 37% -> 41% of each run, Pallas kernels for 0% -> 0%
where the time goes in v1:
time: 223 us; the launch traced here: 221 us
  local copies, waits for them, and re-layouts  75.4 us (34%)
  blocking collectives  42.4 us (19%)
  other arithmetic  31.9 us (14%)
  matrix products  31.6 us (14%)
  between operations  13.8 us (6%)
  starting transfers between devices  11.2 us (5%)
  loops' own time  7.62 us (3%)
  waiting for transfers between devices  7.11 us (3%)
    all_gather x1, blocking collectives, shards(): lax.all_gather(local_summary, ('grp', 'seq'), axis=1, tiled=True)  42.4 us
    dot_general x12, matrix products, attend(): jnp.einsum('bghtn,bgnd->bghtd', rounded, key_block[..., head_dim:], prefe...  17.7 us
    another operation x2, local copies, waits for them, and re-layouts, shards(): by_heads(query_blocks, chosen, allowed_sel, False)  17.5 us
    dot_general x12, matrix products, attend(): jnp.einsum('btghd,bgnd->bghtn', query_block, key_block[..., :head_dim], p...  13.8 us
    dynamic_slice x12, local copies, waits for them, and re-layouts, by_heads(): lax.map(head_slab, jnp.arange(head_count // slab_width, dtype=jnp.int32))  9.94 us
    sub x4, other arithmetic, attend(): weights = jnp.where(allowed_wide, jnp.exp(scores - top_score), 0.0)  8.59 us
    another operation x3, loops' own time, by_heads(): lax.map(head_slab, jnp.arange(head_count // slab_width, dtype=jnp.int32))  7.62 us
    all_to_all x1, waiting for transfers between devices, shards(): lax.all_to_all(local_view[asked_clipped % dev_blocks, :, asked_clipped //...  6.38 us
  transfers between devices with their start and end apart: 6, of which 1 were waited for; matrix products, arithmetic and copies ran while one was open for 41% of the time, Pallas kernels for 0%

profile of v1, /device:TPU:0, one launch (start us, length us, event | category | flops | bytes accessed | tf_op | source)
XLA Modules:
  0.0 221.0 jit_solution(15610906751082634305)
XLA Ops:
  12.1 3.0 %collective-permute-start = (s32[1,2]{0,1:T(2,128)}, s32[1,2]{0,1:T(2,128)}, u32[]{:S(2)}, u32[]{:S(2)}) collective-permute-start(s32[1,2]{0,1:T(2,128)} %get-tuple-element.300), channel_id=1, source_target_pairs={{0,8},{8,0},{16,24},{24,16},{1,9},{9,1},{17,25},{25,17},{2,10},{10... | collective-permute-start | bytes 32 | tf_op jit(solution)/shard_map/ppermute | solution.py:36
  15.1 2.6 %collective-permute-start.1 = (s32[1,2]{0,1:T(2,128)}, s32[1,2]{0,1:T(2,128)}, u32[]{:S(2)}, u32[]{:S(2)}) collective-permute-start(s32[1,2]{0,1:T(2,128)} %get-tuple-element.299), channel_id=1, source_target_pairs={{0,16},{8,24},{16,0},{24,8},{1,17},{9,25},{17,1},{25,9},{2,18},{10... | collective-permute-start | bytes 32 | tf_op jit(solution)/shard_map/ppermute | solution.py:36
  18.8 2.6 %copy.91 = bf16[128,6144]{0,1:T(8,128)(2,1)} copy(bf16[128,6144]{1,0:T(8,128)(2,1)} %param.12) | data formatting | bytes 3145728 | tf_op args[0]
  21.9 42.4 %all_gather.6 = bf16[2,64,384]{2,0,1:T(2,128)(2,1)S(1)} all-gather(bf16[2,2,384]{2,0,1:T(2,128)(2,1)S(1)} %bitcast.261), channel_id=1, replica_groups=mesh['grp'=4,'seq'=8] {'grp','seq'}, dimensions={1}, use_global_device_ids=true | all-gather | bytes 101376 | tf_op jit(solution)/shard_map/all_gather | solution.py:146
  65.1 14.9 %while.33 = (s32[]{:T(128)}, f32[4,1,128,2,4,192]{2,5,4,0,3,1:T(8,128)S(1)}, s32[4]{0:T(128)}, bf16[1,128,2,16,192]{1,4,3,2,0:T(8,128)(2,1)}, bf16[1,2,64,384]{3...) while((s32[]{:T(128)}, ...), condition=%wide.region_4.5_spmd.clone, body=%wide.region_1.4_spmd.clone.sunk | while | flops 51128324 | bytes 2171823 | solution.py:89
  80.8 1.8 copy.101
  91.6 2.3 %gather_fusion.2 = bf16[8,64,384]{2,1,0:T(8,128)(2,1)} fusion(bf16[2,64,2,384]{3,1,2,0:T(8,128)(2,1)} %copy.101, s32[8]{0:T(128)S(1)} %reshape.571), kind=kCustom, calls=%fused_computation.2 | custom fusion | bytes 786496 | tf_op jit(solution)/shard_map/gather | solution.py:158
  93.9 3.5 %all-to-all-start = ((bf16[4,2,64,384]{3,2,1,0:T(8,128)(2,1)}), bf16[4,2,64,384]{3,2,1,0:T(8,128)(2,1)S(1)}, u32[]{:S(2)}, u32[]{:S(2)}) async-start(bf16[4,2,64,384]{3,2,1,0:T(8,128)(2,1)} %bitcast.254), calls=%async_computation | async-start | bytes 786432 | tf_op jit(solution)/shard_map/all_to_all | solution.py:157
  98.1 4.7 %reshape.551 = bf16[2,64,2,16,192]{4,3,2,1,0:T(8,128)(2,1)} reshape(bf16[128,6144]{1,0:T(8,128)(2,1)} %param.12) | data formatting | bytes 3145728 | tf_op jit(solution)/shard_map/reshape | solution.py:186
  103.4 6.4 %all-to-all-done = bf16[4,2,64,384]{3,2,1,0:T(8,128)(2,1)S(1)} async-done(((bf16[4,2,64,384]{3,2,1,0:T(8,128)(2,1)}), bf16[4,2,64,384]{3,2,1,0:T(8,128)(2,1)S(1)}, u32[]{:S(2)}, u32[]{:S(2)}) %all-to-all-start) | async-done | bytes 393248 | tf_op jit(solution)/shard_map/all_to_all | solution.py:157
  109.8 2.7 %gather_fusion.3 = bf16[64,64,384]{2,1,0:T(8,128)(2,1)} fusion(bf16[4,2,64,384]{3,2,1,0:T(8,128)(2,1)S(1)} %all-to-all-done, s32[64]{0:T(128)S(1)} %reshape.577), kind=kCustom, calls=%fused_computation.3 | custom fusion | bytes 6291968 | tf_op jit(solution)/shard_map/gather | solution.py:166
  112.5 3.4 %reshape.552 = bf16[16,64,2,384]{3,2,1,0:T(2,128)(2,1)S(1)} reshape(bf16[1024,768]{1,0:T(8,128)(2,1)} %all-gather.2.cloned.1.call-done) | data formatting | bytes 3145728 | tf_op jit(solution)/shard_map/reshape | solution.py:169
  116.2 2.7 %gather_fusion = bf16[64,64,384]{2,1,0:T(8,128)(2,1)} fusion(bf16[16,64,2,384]{3,1,2,0:T(8,128)(2,1)S(1)} %copy.94, s32[64]{0:T(128)S(1)} %reshape.555), kind=kCustom, calls=%fused_computation | custom fusion | bytes 6291968 | tf_op jit(solution)/shard_map/gather | solution.py:170
  118.9 4.4 %broadcast_select_fusion = bf16[2,2,1024,384]{3,2,1,0:T(8,128)(2,1)} fusion(bf16[2,2,1024,384]{3,2,1,0:T(8,128)(2,1)} %bitcast.252, bf16[2,2,1024,384]{3,2,1,0:T(8,128)(2,1)} %bitcast.251, pred[2,2,1024]{2,1,0:T(4,128)(4,1)S(1)} %broadcast_in_dim.162), kind=kLoop, calls=%fused_computation.85 | loop fusion | flops 1572864 | bytes 9441280 | tf_op jit(solution)/shard_map/jit(_where)/select_n | solution.py:175
  123.3 3.2 %copy.103 = bf16[2,2,1024,384]{2,3,1,0:T(8,128)(2,1)S(1)} copy(bf16[2,2,1024,384]{3,2,1,0:T(8,128)(2,1)} %broadcast_select_fusion) | data formatting | bytes 6291456
  128.1 2.1 collective-permute-start.3
  130.2 30.6 %while.34 = (s32[]{:T(128)}, f32[4,2,64,2,4,192]{5,2,4,3,1,0:T(8,128)}, s32[4]{0:T(128)S(1)}, bf16[2,64,2,16,192]{4,3,2,1,0:T(8,128)(2,1)}, bf16[2,2,1024,384]{2...) while((s32[]{:T(128)}, ...), condition=%wide.region_12.13_spmd.clone, body=%wide.region_9.12_spmd.clone.sunk | while | flops 814416896 | bytes 18646196 | solution.py:89
  133.9 2.1 fusion.134
  141.6 2.1 fusion.134
  149.2 2.1 fusion.134
  156.9 2.1 fusion.134
  160.8 11.7 %copy.116 = f32[2,64,2,4,4,192]{1,0,5,4,3,2:T(2,128)} copy(f32[2,64,2,4,4,192]{5,1,4,2,0,3:T(8,128)} %bitcast.17) | data formatting | bytes 6291456 | tf_op jit(solution)/shard_map/reshape;reshape | solution.py:187
  172.5 5.8 %reshape.611 = f32[128,6144]{0,1:T(8,128)S(1)} reshape(f32[2,64,2,4,4,192]{1,0,5,4,3,2:T(2,128)} %copy.116) | data formatting | bytes 6291456 | tf_op jit(solution)/shard_map/reshape;reshape | solution.py:187
  181.1 1.9 copy.106
  183.0 2.0 broadcast.674.clone2
  185.1 21.9 %while.35 = (s32[]{:T(128)}, f32[4,1,128,2,4,192]{2,5,4,0,3,1:T(8,128)}, s32[4]{0:T(128)S(1)}, bf16[1,128,2,16,192]{1,4,3,2,0:T(8,128)(2,1)}, bf16[1,2,256,384]{...) while((s32[]{:T(128)}, ...), condition=%wide.region_16.17_spmd.clone, body=%wide.region_13.16_spmd.clone.sunk | while | flops 204011520 | bytes 4873147 | solution.py:89
  188.3 2.2 %fusion.140 = f32[4,1,128,2,4,192]{2,5,4,0,3,1:T(8,128)} fusion(f32[4,1,128,2,4,192]{2,5,4,0,3,1:T(8,128)} %get-tuple-element.479, s32[]{:T(128)} %get-tuple-element.478, f32[1,2,4,128,256]{4,3,2,1,0:T(8,128)S(1)} %get-tuple-element.463, f32[2,4,128]{2,1,0:T(4,128)S(1)} %get-tuple-element.464, pred[128,256]{1,0:T(8,128)(4,1)S(1)} %and_and_fusion.2, ...), kind=kOutput, calls=%fused_computation.61.clone.1 | convolution fusion | flops 101646336 | bytes 2073088 | tf_op jit(solution)/shard_map/while/body/eval_jaxpr/bghtn,bgnd->bghtd/dot_general | solution.py:70
  193.8 2.2 %fusion.140 = f32[4,1,128,2,4,192]{2,5,4,0,3,1:T(8,128)} fusion(f32[4,1,128,2,4,192]{2,5,4,0,3,1:T(8,128)} %get-tuple-element.479, s32[]{:T(128)} %get-tuple-element.478, f32[1,2,4,128,256]{4,3,2,1,0:T(8,128)S(1)} %get-tuple-element.463, f32[2,4,128]{2,1,0:T(4,128)S(1)} %get-tuple-element.464, pred[128,256]{1,0:T(8,128)(4,1)S(1)} %and_and_fusion.2, ...), kind=kOutput, calls=%fused_computation.61.clone.1 | convolution fusion | flops 101646336 | bytes 2073088 | tf_op jit(solution)/shard_map/while/body/eval_jaxpr/bghtn,bgnd->bghtd/dot_general | solution.py:70
  199.2 2.2 %fusion.140 = f32[4,1,128,2,4,192]{2,5,4,0,3,1:T(8,128)} fusion(f32[4,1,128,2,4,192]{2,5,4,0,3,1:T(8,128)} %get-tuple-element.479, s32[]{:T(128)} %get-tuple-element.478, f32[1,2,4,128,256]{4,3,2,1,0:T(8,128)S(1)} %get-tuple-element.463, f32[2,4,128]{2,1,0:T(4,128)S(1)} %get-tuple-element.464, pred[128,256]{1,0:T(8,128)(4,1)S(1)} %and_and_fusion.2, ...), kind=kOutput, calls=%fused_computation.61.clone.1 | convolution fusion | flops 101646336 | bytes 2073088 | tf_op jit(solution)/shard_map/while/body/eval_jaxpr/bghtn,bgnd->bghtd/dot_general | solution.py:70
  204.7 2.3 %fusion.140 = f32[4,1,128,2,4,192]{2,5,4,0,3,1:T(8,128)} fusion(f32[4,1,128,2,4,192]{2,5,4,0,3,1:T(8,128)} %get-tuple-element.479, s32[]{:T(128)} %get-tuple-element.478, f32[1,2,4,128,256]{4,3,2,1,0:T(8,128)S(1)} %get-tuple-element.463, f32[2,4,128]{2,1,0:T(4,128)S(1)} %get-tuple-element.464, pred[128,256]{1,0:T(8,128)(4,1)S(1)} %and_and_fusion.2, ...), kind=kOutput, calls=%fused_computation.61.clone.1 | convolution fusion | flops 101646336 | bytes 2073088 | tf_op jit(solution)/shard_map/while/body/eval_jaxpr/bghtn,bgnd->bghtd/dot_general | solution.py:70
  207.0 4.6 %fusion.84 = bf16[128,6144]{0,1:T(8,128)(2,1)} fusion(f32[4,1,128,2,4,192]{2,5,4,0,3,1:T(8,128)} %get-tuple-element.103, f32[4,1,128,2,4,192]{2,5,4,0,3,1:T(8,128)} %copy-done.1, f32[128,6144]{0,1:T(8,128)S(1)} %reshape.611, f32[128,2,16]{0,2,1:T(8,128)S(1)} %bitcast.259, f32[128,2,16]{0,2,1:T(8,128)S(1)} %bitcast.260, f32[128,2,16]{0,2,1:T(8,128)S(1)} %bitcast.258), kind=kLoop, calls=%fused_computation.81 | loop fusion | flops 4718592 | bytes 11059200 | tf_op jit(solution)/shard_map/convert_element_type | solution.py:213
  211.6 2.6 %copy.108 = bf16[128,6144]{1,0:T(8,128)(2,1)} copy(bf16[128,6144]{0,1:T(8,128)(2,1)} %fusion.84) | data formatting | bytes 3145728 | tf_op jit(solution)/shard_map/convert_element_type | solution.py:213
  (170 shorter events, 65.7 us)
Async XLA Ops:
  6.5 15.1 %copy-start = (bf16[384,384]{1,0:T(8,128)(2,1)S(1)}, bf16[384,384]{1,0:T(8,128)(2,1)}, u32[]{:S(2)}) copy-start(bf16[384,384]{1,0:T(8,128)(2,1)} %param.17) | copy-start | bytes 884740
  6.5 14.9 %copy-start.3 = (bf16[64,384]{1,0:T(8,128)(2,1)S(1)}, bf16[64,384]{1,0:T(8,128)(2,1)}, u32[]{:S(2)}) copy-start(bf16[64,384]{1,0:T(8,128)(2,1)} %param.16) | copy-start | bytes 147460
  6.5 106.0 %all-gather.2.cloned.1.call-start = ((), (), s32[]{:S(2)}) async-start(), calls=%async_computation.1 | async-start | bytes 1769472 | tf_op jit(solution)/shard_map/all_gather | solution.py:167
  9.7 8.0 %copy-start.7 = (pred[2,32]{1,0:T(4,128)(4,1)}, pred[2,32]{1,0:T(4,128)(4,1)S(1)}, u32[]{:S(2)}) copy-start(pred[2,32]{1,0:T(4,128)(4,1)S(1)} %get-tuple-element.301) | copy-start | bytes 196
  9.7 8.0 %copy-start.8 = (pred[2,32]{1,0:T(4,128)(4,1)}, pred[2,32]{1,0:T(4,128)(4,1)S(1)}, u32[]{:S(2)}) copy-start(pred[2,32]{1,0:T(4,128)(4,1)S(1)} %get-tuple-element.278) | copy-start | bytes 196
  10.2 11.6 %copy-start.5 = (pred[64,4]{0,1:T(4,128)(4,1)}, pred[64,4]{0,1:T(4,128)(4,1)S(1)}, u32[]{:S(2)}) copy-start(pred[64,4]{0,1:T(4,128)(4,1)S(1)} %get-tuple-element.302) | copy-start | bytes 772
  10.2 11.6 %copy-start.6 = (pred[64,4]{0,1:T(4,128)(4,1)}, pred[64,4]{0,1:T(4,128)(4,1)S(1)}, u32[]{:S(2)}) copy-start(pred[64,4]{0,1:T(4,128)(4,1)S(1)} %get-tuple-element.303) | copy-start | bytes 772
  12.1 75.4 %collective-permute-start = (s32[1,2]{0,1:T(2,128)}, s32[1,2]{0,1:T(2,128)}, u32[]{:S(2)}, u32[]{:S(2)}) collective-permute-start(s32[1,2]{0,1:T(2,128)} %get-tuple-element.300), channel_id=1, source_target_pairs={{0,8},{8,0},{16,24},{24,16},{1,9},{9,1},{17,25},{25,17},{2,10},{10... | collective-permute-start | bytes 32 | tf_op jit(solution)/shard_map/ppermute | solution.py:36
  15.1 73.2 %collective-permute-start.1 = (s32[1,2]{0,1:T(2,128)}, s32[1,2]{0,1:T(2,128)}, u32[]{:S(2)}, u32[]{:S(2)}) collective-permute-start(s32[1,2]{0,1:T(2,128)} %get-tuple-element.299), channel_id=1, source_target_pairs={{0,16},{8,24},{16,0},{24,8},{1,17},{9,25},{17,1},{25,9},{2,18},{10... | collective-permute-start | bytes 32 | tf_op jit(solution)/shard_map/ppermute | solution.py:36
  17.7 71.4 %collective-permute-start.2 = (s32[1,2]{0,1:T(2,128)}, s32[1,2]{0,1:T(2,128)}, u32[]{:S(2)}, u32[]{:S(2)}) collective-permute-start(s32[1,2]{0,1:T(2,128)} %get-tuple-element.298), channel_id=1, source_target_pairs={{0,24},{8,16},{16,8},{24,0},{1,25},{9,17},{17,9},{25,1},{2,26},{10... | collective-permute-start | bytes 32 | tf_op jit(solution)/shard_map/ppermute | solution.py:36
  18.7 45.5 %copy-start.2 = (bf16[2,64,2,384]{3,2,1,0:T(2,128)(2,1)}, bf16[2,64,2,384]{3,2,1,0:T(2,128)(2,1)S(1)}, u32[]{:S(2)}) copy-start(bf16[2,64,2,384]{3,2,1,0:T(2,128)(2,1)S(1)} %reshape.549) | copy-start | bytes 589828
  80.0 14.0 %copy-start.1 = (f32[4,1,128,2,4,192]{2,5,4,0,3,1:T(8,128)}, f32[4,1,128,2,4,192]{2,5,4,0,3,1:T(8,128)S(1)}, u32[]{:S(2)}) copy-start(f32[4,1,128,2,4,192]{2,5,4,0,3,1:T(8,128)S(1)} %get-tuple-element.101) | copy-start | bytes 9437188
  80.0 23.4 %copy-start.4 = (bf16[3,128,32]{1,2,0:T(8,128)(2,1)S(1)}, bf16[3,128,32]{1,2,0:T(8,128)(2,1)}, u32[]{:S(2)}) copy-start(bf16[3,128,32]{1,2,0:T(8,128)(2,1)} %param.15) | copy-start | bytes 73732
  93.9 15.9 %all-to-all-start = ((bf16[4,2,64,384]{3,2,1,0:T(8,128)(2,1)}), bf16[4,2,64,384]{3,2,1,0:T(8,128)(2,1)S(1)}, u32[]{:S(2)}, u32[]{:S(2)}) async-start(bf16[4,2,64,384]{3,2,1,0:T(8,128)(2,1)} %bitcast.254), calls=%async_computation | async-start | bytes 786432 | tf_op jit(solution)/shard_map/all_to_all | solution.py:157
  128.1 50.2 %collective-permute-start.3 = (bf16[128,768]{1,0:T(8,128)(2,1)}, bf16[128,768]{1,0:T(8,128)(2,1)}, u32[]{:S(2)}, u32[]{:S(2)}) collective-permute-start(bf16[128,768]{1,0:T(8,128)(2,1)} %slice.54), channel_id=1, source_target_pairs={{0,8},{8,16},{16,24},{1,9},{9,17},{17,25},{2,10},{10,18},{18,26},{... | collective-permute-start | bytes 589832 | tf_op jit(solution)/shard_map/ppermute | solution.py:44
Sparse Core Ops, SparseCore 0:
  9.2 28.5 all-gather.1
